TPU v7x, 256 devices: a whole 4x4x8 slice. The times are simulated.
256 devices in a mesh: seq: 8 (over z), sub: 32 (over y, x, core).
Axes of the slice: x: 4, y: 4, z: 8, core: 2. Of those that a mesh axis runs over, the one named last changes fastest.
Arguments:
- queries: bfloat16 [65536, 512], P(('seq', 'sub')), may hold values from -7 to 7
- keys: bfloat16 [65536, 512], P(('seq', 'sub')), may hold values from -7 to 7
- values: bfloat16 [65536, 512], P(('seq', 'sub')), may hold values from -7 to 7
- cotangent: bfloat16 [65536, 512], P(('seq', 'sub')), may hold values from -6 to 6
Outputs:
- attention: bfloat16 [65536, 512], P(('seq', 'sub'))
- query_grad: bfloat16 [65536, 512], P(('seq', 'sub'))
- key_grad: bfloat16 [65536, 512], P(('seq', 'sub'))
- value_grad: bfloat16 [65536, 512], P(('seq', 'sub'))
All inputs are finite; a program needn't handle non-finite values.
Results may differ from a plain program's by a relative error of at most 0.01.
Values may be sent and summed in bfloat16 or wider, within the bound.
A program may use at most 128 MiB of HBM per device.

v0:
```python
import functools
import math

import jax
import jax.numpy as jnp
from jax import lax
from jax.experimental import pallas as pl
from jax.experimental.pallas import tpu as pltpu
from jax.sharding import PartitionSpec as P

MESH = pl.DeviceIdType.MESH
HEADS = 8
HEAD = 64
BLOCK = 256
FEATURES = 512
LEVELS = 4
PAIRS = HEADS // 2
NEAR_UNITS = 3
KEYS = 3 * BLOCK + 3 * LEVELS * 128
CONTRIBUTIONS = 256 + 3 * 192
OUTSIDE = 1e30
bf16 = jnp.bfloat16
f32 = jnp.float32

OWN, LEFT, RIGHT = 0, 1, 2


def dot_nt(a, b):
    return lax.dot_general(a, b, (((1,), (1,)), ((), ())), preferred_element_type=f32)


def dot_nn(a, b):
    return lax.dot_general(a, b, (((1,), (0,)), ((), ())), preferred_element_type=f32)


def level_rows(level):
    return BLOCK >> level


def unit_offset(unit):
    return unit * BLOCK if unit < NEAR_UNITS else 3 * BLOCK + (unit - NEAR_UNITS) * 384


def contribution_base(level):
    return 0 if level == 1 else 256 + (level - 2) * 192


def kernel(
    device_count,
    sub_count,
    q_ref, k_ref, v_ref, g_ref,
    att_ref, dq_ref, dk_ref, dv_ref,
    near, lev1, lev2, lev3, lev4, pieces,
    qm, gm, gt, kt, prob, top, unit_top, total, ot, dqt, factor, delta,
    eye, upsample, average,
    near_grad, own_grad, piece_grad, twin_grad, twin_third, near_in, coarse_in,
    near_send, near_recv, plane_send, plane_recv, twin_send, twin_recv,
    gnear_send, gnear_recv, gplane_send, gplane_recv, gtwin_send, gtwin_recv,
):
    n = device_count
    me = lax.axis_index("seq") * sub_count + lax.axis_index("sub")
    core = lax.rem(me, 2)
    twin = me + 1 - 2 * core
    levels = [lev1, lev2, lev3, lev4]

    def wrapped(device):
        return lax.rem(device + n, n)

    def mesh_id(device):
        return (device // sub_count, lax.rem(device, sub_count))

    def group_size(level):
        return 2 ** (level - 1)

    def chips(level):
        return max(group_size(level) // 2, 1)

    def chip_place(level):
        return lax.rem(me // 2, chips(level))

    def group_targets(level):
        size = group_size(level)
        group = me // size
        count = n // size
        odd = lax.rem(group, 2)
        third = lax.rem(group + 3 - 6 * odd + count, count)
        below = lax.rem(group - 2 + count, count)
        above = lax.rem(group + 2, count)
        return [below * size, above * size, third * size]

    def plane_target(level, start, chip):
        if level == 1:
            return start
        return start + 2 * chip + core

    partners = [twin, wrapped(me - 1 + 2 * core)]
    for level in range(1, LEVELS + 1):
        starts = group_targets(level)[: 2 if level == 1 else 3]
        for start in starts:
            for chip in range(chips(level)):
                partners.append(plane_target(level, start, chip))

    barrier = pltpu.get_barrier_semaphore()
    for partner in partners:
        pl.semaphore_signal(barrier, inc=1, device_id=mesh_id(partner), device_id_type=MESH)

    row = lax.broadcasted_iota(jnp.int32, (BLOCK, BLOCK), 0)
    col = lax.broadcasted_iota(jnp.int32, (BLOCK, BLOCK), 1)
    eye[...] = jnp.where(row == col, 1.0, 0.0).astype(bf16)
    average[...] = jnp.where(row[:128] == col[:128] // 2, 0.5, 0.0).astype(bf16)
    near[OWN, 0] = k_ref[...]
    near[OWN, 1] = v_ref[...]
    for kv in range(2):
        lev1[kv] = dot_nn(average[...], near[OWN, kv]).astype(bf16)
    for level in range(2, LEVELS + 1):
        fine, coarse = levels[level - 2], levels[level - 1]
        rows = level_rows(level)
        for kv in range(2):
            coarse[kv] = dot_nn(average[:rows, : 2 * rows], fine[kv]).astype(bf16)

    pl.semaphore_wait(barrier, len(partners))

    started = []

    def remote(src, dst, send, recv, device):
        copy = pltpu.make_async_remote_copy(
            src_ref=src, dst_ref=dst, send_sem=send, recv_sem=recv,
            device_id=mesh_id(device), device_id_type=MESH,
        )
        copy.start()
        started.append(copy)

    def arrived(ref, sem):
        pltpu.make_async_copy(ref, ref, sem).wait()

    place = 0
    for level in range(LEVELS, 1, -1):
        rows = level_rows(level)
        targets = group_targets(level)
        for slot, start in ((1, targets[0]), (0, targets[1]), (2, targets[2])):
            for chip in range(chips(level)):
                offset = pl.multiple_of(core * 64 + chip_place(level) * rows, 16)
                remote(
                    levels[level - 1],
                    pieces.at[level - 1, slot, :, pl.ds(offset, rows)],
                    plane_send.at[place],
                    plane_recv.at[3 * (level - 1) + slot],
                    plane_target(level, start, chip),
                )
                place += 1
    targets = group_targets(1)
    for slot, start in ((1, targets[0]), (0, targets[1])):
        remote(lev1, pieces.at[0, slot], plane_send.at[place], plane_recv.at[slot], start)
        place += 1
    remote(near.at[OWN], near.at[LEFT], near_send.at[0], near_recv.at[LEFT], wrapped(me + 1))
    remote(near.at[OWN], near.at[RIGHT], near_send.at[1], near_recv.at[RIGHT], wrapped(me - 1))

    lane = lax.broadcasted_iota(jnp.int32, (BLOCK, 128), 1)

    def prepare(pair, carry):
        lanes = pl.ds(pl.multiple_of(pair * 128, 128), 128)
        queries = q_ref[:, lanes].astype(f32) * (1.0 / math.sqrt(HEAD))
        grads = g_ref[:, lanes]
        grads_wide = grads.astype(f32)
        for half in range(2):
            mine = (lane >= 64) if half else (lane < 64)
            qm[2 * pair + half] = jnp.where(mine, queries, 0.0).astype(bf16)
            gm[2 * pair + half] = jnp.where(mine, grads_wide, 0.0).astype(bf16)
        gt[pair] = dot_nt(eye[:128, :128], grads)
        return carry

    lax.fori_loop(0, PAIRS, prepare, 0)

    def forward(load, size, valid, offset, unit, first=False):
        parts = len(valid)
        step = size // parts

        def body(pair, carry):
            lanes = pl.ds(pl.multiple_of(pair * 128, 128), 128)
            keys, values = load(0, lanes), load(1, lanes)
            kt[lanes, offset : offset + size] = dot_nt(eye[:128, :128], keys).astype(bf16)
            values_t = dot_nt(eye[:128, :128], values).astype(bf16)
            for half in range(2):
                head = 2 * pair + half
                scores = dot_nt(keys, qm[head])
                blocks = [scores[i * step : (i + 1) * step] for i in range(parts)]
                high = None
                for block, flag in zip(blocks, valid):
                    peak = jnp.max(block, axis=0, keepdims=True)
                    if flag is not None:
                        peak = jnp.where(flag, peak, -OUTSIDE)
                    high = peak if high is None else jnp.maximum(high, peak)
                if not first:
                    before = top[head]
                    high = jnp.maximum(high, before)
                weights, sums = [], None
                for block, flag in zip(blocks, valid):
                    shift = high if flag is None else jnp.where(flag, high, OUTSIDE)
                    weight = jnp.exp(block - shift)
                    added = jnp.sum(weight, axis=0, keepdims=True)
                    sums = added if sums is None else sums + added
                    weights.append(weight.astype(bf16))
                weight = weights[0] if parts == 1 else jnp.concatenate(weights, axis=0)
                prob[head, offset : offset + size] = weight
                part = dot_nn(values_t[half * 64 : half * 64 + 64], weight)
                if first:
                    total[head] = sums
                    ot[head] = part
                else:
                    fade = jnp.exp(before - high)
                    total[head] = total[head] * fade + sums
                    ot[head] = ot[head] * fade + part
                top[head] = high
                unit_top[unit, head] = high
            return carry

        lax.fori_loop(0, PAIRS, body, 0)

    def near_load(slot):
        return lambda kv, lanes: near[slot, kv, :, lanes]

    def piece_load(level):
        return lambda kv, lanes: jnp.concatenate(
            [pieces[level - 1, slot, kv, :, lanes] for slot in range(3)], axis=0
        )

    far_slot = LEFT + core
    twin_slot = RIGHT - core
    far_valid = jnp.logical_or(
        jnp.logical_and(core == 0, me >= 1), jnp.logical_and(core == 1, me < n - 1)
    )
    level_valid = {}
    for level in range(1, LEVELS + 1):
        size = group_size(level)
        group, count = me // size, n // size
        odd = lax.rem(group, 2)
        third = group + 3 - 6 * odd
        level_valid[level] = [
            group >= 2,
            group + 2 < count,
            jnp.logical_and(third >= 0, third < count),
        ]

    half_rows = pl.ds(pl.multiple_of(core * 64, 64), 64)
    other_rows = pl.ds(pl.multiple_of(64 - core * 64, 64), 64)

    def plane_arrived(level):
        for slot in range(3):
            arrived(
                pieces.at[level - 1, slot, :, half_rows], plane_recv.at[3 * (level - 1) + slot]
            )

    def to_twin(level):
        for slot in range(3):
            ref = pieces.at[level - 1, slot, :, half_rows]
            at = 3 * (level - 1) + slot
            remote(ref, ref, twin_send.at[at], twin_recv.at[at], twin)

    def twin_arrived(level):
        for slot in range(3):
            arrived(
                pieces.at[level - 1, slot, :, other_rows], twin_recv.at[3 * (level - 1) + slot]
            )

    def forward_level(level):
        unit = NEAR_UNITS + level - 1
        forward(piece_load(level), 384, level_valid[level], unit_offset(unit), unit)

    forward(near_load(OWN), BLOCK, [None], unit_offset(0), 0, first=True)
    arrived(near.at[twin_slot], near_recv.at[twin_slot])
    forward(near_load(twin_slot), BLOCK, [None], unit_offset(1), 1)
    plane_arrived(4)
    to_twin(4)
    plane_arrived(3)
    to_twin(3)
    twin_arrived(4)
    forward_level(4)
    plane_arrived(2)
    to_twin(2)
    twin_arrived(3)
    forward_level(3)
    arrived(pieces.at[0, 0], plane_recv.at[0])
    arrived(pieces.at[0, 1], plane_recv.at[1])
    remote(pieces.at[0, core], pieces.at[0, 2], twin_send.at[0], twin_recv.at[0], twin)
    twin_arrived(2)
    forward_level(2)
    arrived(pieces.at[0, 2], twin_recv.at[0])
    forward_level(1)
    arrived(near.at[far_slot], near_recv.at[far_slot])
    forward(near_load(far_slot), BLOCK, [far_valid], unit_offset(2), 2)

    def finish(pair, carry):
        lanes = pl.ds(pl.multiple_of(pair * 128, 128), 128)
        outs = []
        for half in range(2):
            head = 2 * pair + half
            scale = 1.0 / total[head]
            out = ot[head] * scale
            outs.append(out.astype(bf16))
            delta[head] = jnp.sum(
                gt[pair, half * 64 : half * 64 + 64] * out, axis=0, keepdims=True
            )
            high = top[head]
            for unit in range(NEAR_UNITS + LEVELS):
                factor[unit, head] = jnp.exp(unit_top[unit, head] - high) * scale
            dqt[head] = jnp.zeros((HEAD, BLOCK), f32)
        att_ref[:, lanes] = dot_nt(eye[...], jnp.concatenate(outs, axis=0)).astype(bf16)
        return carry

    lax.fori_loop(0, PAIRS, finish, 0)

    def backward(load, size, offset, unit, store):
        def body(pair, carry):
            lanes = pl.ds(pl.multiple_of(pair * 128, 128), 128)
            values = load(1, lanes)
            key_part, value_part = None, None
            for half in range(2):
                head = 2 * pair + half
                wide = prob[head, offset : offset + size].astype(f32) * factor[unit, head]
                dscore = (wide * (dot_nt(values, gm[head]) - delta[head])).astype(bf16)
                key_new = dot_nn(dscore, qm[head])
                value_new = dot_nn(wide.astype(bf16), gm[head])
                key_part = key_new if key_part is None else key_part + key_new
                value_part = value_new if value_part is None else value_part + value_new
                rows = pl.ds(pl.multiple_of(pair * 128 + half * 64, 64), 64)
                dqt[head] += dot_nn(kt[rows, offset : offset + size], dscore)
            store(lanes, key_part, value_part)
            return carry

        lax.fori_loop(0, PAIRS, body, 0)

    def near_store(slot):
        def store(lanes, key_part, value_part):
            near_grad[slot, 0, :, lanes] = key_part.astype(bf16)
            near_grad[slot, 1, :, lanes] = value_part.astype(bf16)
        return store

    def own_store(lanes, key_part, value_part):
        own_grad[0, :, lanes] = key_part
        own_grad[1, :, lanes] = value_part

    def piece_store(level):
        def store(lanes, key_part, value_part):
            for slot in range(3):
                at = slice(slot * 128, slot * 128 + 128)
                piece_grad[level - 1, slot, 0, :, lanes] = key_part[at].astype(bf16)
                piece_grad[level - 1, slot, 1, :, lanes] = value_part[at].astype(bf16)
        return store

    def backward_level(level):
        unit = NEAR_UNITS + level - 1
        backward(piece_load(level), 384, unit_offset(unit), unit, piece_store(level))

    def grads_to_twin(level):
        for slot in range(3):
            at = 3 * (level - 1) + slot
            remote(
                piece_grad.at[level - 1, slot, :, other_rows],
                twin_grad.at[level - 2, slot],
                gtwin_send.at[at], gtwin_recv.at[at], twin,
            )

    def grads_to_owners(level, place):
        rows = level_rows(level)
        for slot in range(3):
            arrived(twin_grad.at[level - 2, slot], gtwin_recv.at[3 * (level - 1) + slot])
            for kv in range(2):
                piece_grad[level - 1, slot, kv, half_rows] = (
                    piece_grad[level - 1, slot, kv, half_rows].astype(f32)
                    + twin_grad[level - 2, slot, kv].astype(f32)
                ).astype(bf16)
        targets = group_targets(level)
        for slot in range(3):
            for chip in range(chips(level)):
                source = pl.multiple_of(core * 64 + chip * rows, 16)
                base = contribution_base(level) + slot * 64
                target = pl.multiple_of(base + chip_place(level) * rows, 16)
                remote(
                    piece_grad.at[level - 1, slot, :, pl.ds(source, rows)],
                    coarse_in.at[:, pl.ds(target, rows)],
                    gplane_send.at[place], gplane_recv.at[level - 1],
                    plane_target(level, targets[slot], chip),
                )
                place += 1
        return place

    backward(near_load(far_slot), BLOCK, unit_offset(2), 2, near_store(1))
    far_device = wrapped(me - 1 + 2 * core)
    remote(near_grad.at[1], near_in.at[1], gnear_send.at[1], gnear_recv.at[1], far_device)
    backward_level(4)
    grads_to_twin(4)
    backward_level(3)
    grads_to_twin(3)
    place = grads_to_owners(4, 0)
    backward_level(2)
    grads_to_twin(2)
    place = grads_to_owners(3, place)
    backward_level(1)
    remote(piece_grad.at[0, 2], twin_third, gtwin_send.at[0], gtwin_recv.at[0], twin)
    place = grads_to_owners(2, place)
    arrived(twin_third, gtwin_recv.at[0])
    for kv in range(2):
        piece_grad[0, core, kv] = (
            piece_grad[0, core, kv].astype(f32) + twin_third[kv].astype(f32)
        ).astype(bf16)
    targets = group_targets(1)
    for slot in range(2):
        remote(
            piece_grad.at[0, slot], coarse_in.at[:, pl.ds(slot * 128, 128)],
            gplane_send.at[place], gplane_recv.at[0], targets[slot],
        )
        place += 1
    backward(near_load(twin_slot), BLOCK, unit_offset(1), 1, near_store(0))
    remote(near_grad.at[0], near_in.at[0], gnear_send.at[0], gnear_recv.at[0], twin)
    backward(near_load(OWN), BLOCK, unit_offset(0), 0, own_store)

    def write_queries(pair, carry):
        lanes = pl.ds(pl.multiple_of(pair * 128, 128), 128)
        both = jnp.concatenate([dqt[2 * pair], dqt[2 * pair + 1]], axis=0)
        both = (both * (1.0 / math.sqrt(HEAD))).astype(bf16)
        dq_ref[:, lanes] = dot_nt(eye[...], both).astype(bf16)
        return carry

    lax.fori_loop(0, PAIRS, write_queries, 0)

    for level in range(1, LEVELS + 1):
        count = 128 if level == 1 else level_rows(level)
        base = contribution_base(level)
        width = 256 if level == 1 else 192
        r = lax.broadcasted_iota(jnp.int32, (BLOCK, width), 0)
        c = lax.broadcasted_iota(jnp.int32, (BLOCK, width), 1)
        upsample[:, base : base + width] = jnp.where(
            lax.rem(c, count) == r // 2**level, 0.5**level, 0.0
        ).astype(bf16)
    arrived(near_in.at[0], gnear_recv.at[0])
    arrived(near_in.at[1], gnear_recv.at[1])
    for level in range(LEVELS, 0, -1):
        width = 256 if level == 1 else 192
        arrived(
            coarse_in.at[:, pl.ds(contribution_base(level), width)], gplane_recv.at[level - 1]
        )
    for kv, out_ref in ((0, dk_ref), (1, dv_ref)):
        def write(pair, carry):
            lanes = pl.ds(pl.multiple_of(pair * 128, 128), 128)
            out = own_grad[kv, :, lanes] + near_in[0, kv, :, lanes].astype(f32)
            out = out + near_in[1, kv, :, lanes].astype(f32)
            out = out + dot_nn(upsample[...], coarse_in[kv, :, lanes])
            out_ref[:, lanes] = out.astype(bf16)
            return carry

        lax.fori_loop(0, PAIRS, write, 0)

    for copy in started:
        copy.wait_send()


def on_device(device_count, sub_count, queries, keys, values, cotangent):
    vmem = pl.BlockSpec(memory_space=pltpu.VMEM)
    dma = pltpu.SemaphoreType.DMA
    rows = (BLOCK, FEATURES)
    plane_messages = 2 + 3 + 6 + 12
    scratch = [
        pltpu.VMEM((3, 2) + rows, bf16),
        pltpu.VMEM((2, 128, FEATURES), bf16),
        pltpu.VMEM((2, 64, FEATURES), bf16),
        pltpu.VMEM((2, 32, FEATURES), bf16),
        pltpu.VMEM((2, 16, FEATURES), bf16),
        pltpu.VMEM((LEVELS, 3, 2, 128, FEATURES), bf16),
        pltpu.VMEM((HEADS, BLOCK, 128), bf16),
        pltpu.VMEM((HEADS, BLOCK, 128), bf16),
        pltpu.VMEM((PAIRS, 128, BLOCK), f32),
        pltpu.VMEM((FEATURES, KEYS), bf16),
        pltpu.VMEM((HEADS, KEYS, BLOCK), bf16),
        pltpu.VMEM((HEADS, 1, BLOCK), f32),
        pltpu.VMEM((NEAR_UNITS + LEVELS, HEADS, 1, BLOCK), f32),
        pltpu.VMEM((HEADS, 1, BLOCK), f32),
        pltpu.VMEM((HEADS, HEAD, BLOCK), f32),
        pltpu.VMEM((HEADS, HEAD, BLOCK), f32),
        pltpu.VMEM((NEAR_UNITS + LEVELS, HEADS, 1, BLOCK), f32),
        pltpu.VMEM((HEADS, 1, BLOCK), f32),
        pltpu.VMEM((BLOCK, BLOCK), bf16),
        pltpu.VMEM((BLOCK, CONTRIBUTIONS), bf16),
        pltpu.VMEM((128, BLOCK), bf16),
        pltpu.VMEM((2, 2) + rows, bf16),
        pltpu.VMEM((2,) + rows, f32),
        pltpu.VMEM((LEVELS, 3, 2, 128, FEATURES), bf16),
        pltpu.VMEM((LEVELS - 1, 3, 2, 64, FEATURES), bf16),
        pltpu.VMEM((2, 128, FEATURES), bf16),
        pltpu.VMEM((2, 2) + rows, bf16),
        pltpu.VMEM((2, CONTRIBUTIONS, FEATURES), bf16),
        dma((2,)), dma((3,)),
        dma((plane_messages,)), dma((3 * LEVELS,)),
        dma((3 * LEVELS,)), dma((3 * LEVELS,)),
        dma((2,)), dma((2,)),
        dma((plane_messages,)), dma((LEVELS,)),
        dma((3 * LEVELS,)), dma((3 * LEVELS,)),
    ]
    return pl.pallas_call(
        functools.partial(kernel, device_count, sub_count),
        out_shape=[jax.ShapeDtypeStruct(rows, bf16)] * 4,
        in_specs=[vmem] * 4,
        out_specs=[vmem] * 4,
        scratch_shapes=scratch,
        compiler_params=pltpu.CompilerParams(
            collective_id=0, has_side_effects=True, vmem_limit_bytes=56 * 2**20
        ),
        name="hierarchical_attention",
    )(queries, keys, values, cotangent)


def solution(mesh):
    spec = P(("seq", "sub"), None)
    device_count = mesh.shape["seq"] * mesh.shape["sub"]
    return jax.shard_map(
        functools.partial(on_device, device_count, mesh.shape["sub"]),
        mesh=mesh,
        in_specs=(spec,) * 4,
        out_specs=(spec,) * 4,
        check_vma=False,
    )
```

profile of v0, /device:TPU:33, one launch (start us, length us, event | category | flops | bytes accessed | tf_op | source)
XLA Modules:
  0.0 99.2 jit_solution(17834635235702422767)
XLA Ops:
  0.6 94.0 %hierarchical_attention.1 = (bf16[256,512]{1,0:T(8,128)(2,1)}, bf16[256,512]{1,0:T(8,128)(2,1)}, bf16[256,512]{1,0:T(8,128)(2,1)}, bf16[256,512]{1,0:T(8,128)(2,1)}) custom-call(bf16[256,512]{1,0:T(8,128)(2,1)} %q_ref.1, bf16[256,512]{1,0:T(8,128)(2,1)} %k_ref.1, bf16[256,512]{1,0:T(8,128)(2,1)} %v_ref.1, bf16[256,512]{1,0:T(8,128)(2,1)} %g_ref.1), custom_call_target="tpu_custom_call" | custom-call | tf_op jit(solution)/shard_map/hierarchical_attention/pallas_call | solution.py:498
  94.6 0.0 copy-start.2
  94.6 1.7 %copy.12 = bf16[256,512]{1,0:T(8,128)(2,1)} copy(bf16[256,512]{1,0:T(8,128)(2,1)} %get-tuple-element.8) | data formatting | bytes 524288
  96.4 0.0 copy-done.2
  96.4 0.0 copy-start.1
  96.4 0.7 copy.13
  97.1 0.3 copy-done.1
  97.4 0.0 copy-start
  97.4 0.7 copy.14
  98.1 0.3 copy-done
  98.5 0.7 copy.15
Async XLA Ops:
  94.6 1.7 %copy-start.2 = (bf16[256,512]{1,0:T(8,128)(2,1)S(1)}, bf16[256,512]{1,0:T(8,128)(2,1)}, u32[]{:S(2)}) copy-start(bf16[256,512]{1,0:T(8,128)(2,1)} %get-tuple-element.9) | copy-start | bytes 786436
  96.4 1.0 %copy-start.1 = (bf16[256,512]{1,0:T(8,128)(2,1)S(1)}, bf16[256,512]{1,0:T(8,128)(2,1)}, u32[]{:S(2)}) copy-start(bf16[256,512]{1,0:T(8,128)(2,1)} %get-tuple-element.10) | copy-start | bytes 786436
  97.4 1.0 %copy-start = (bf16[256,512]{1,0:T(8,128)(2,1)S(1)}, bf16[256,512]{1,0:T(8,128)(2,1)}, u32[]{:S(2)}) copy-start(bf16[256,512]{1,0:T(8,128)(2,1)} %get-tuple-element.11) | copy-start | bytes 786436
where the time goes:
time: 99.3 us; the launch traced here: 99.2 us
  Pallas kernels  94 us (95%)
  local copies, waits for them, and re-layouts  4.5 us (5%)
    pallas_call x1, Pallas kernels, on_device(): pl.pallas_call(functools.partial(kernel, device_count, sub_count), out_sh...  94 us
    unnamed x10, local copies, waits for them, and re-layouts  4.5 us

commit v1 on v0

--- a/solution.py
+++ b/solution.py
@@ -29,6 +29,10 @@
     return lax.dot_general(a, b, (((1,), (1,)), ((), ())), preferred_element_type=f32)
 
 
+def dot_tn(a, b):
+    return lax.dot_general(a, b, (((0,), (0,)), ((), ())), preferred_element_type=f32)
+
+
 def dot_nn(a, b):
     return lax.dot_general(a, b, (((1,), (0,)), ((), ())), preferred_element_type=f32)
 
@@ -51,8 +55,8 @@
     q_ref, k_ref, v_ref, g_ref,
     att_ref, dq_ref, dk_ref, dv_ref,
     near, lev1, lev2, lev3, lev4, pieces,
-    qm, gm, gt, kt, prob, top, unit_top, total, ot, dqt, factor, delta,
-    eye, upsample, average,
+    qm, gm, prob, top, total, out_part, dq_part, factor, delta,
+    upsample, average,
     near_grad, own_grad, piece_grad, twin_grad, twin_third, near_in, coarse_in,
     near_send, near_recv, plane_send, plane_recv, twin_send, twin_recv,
     gnear_send, gnear_recv, gplane_send, gplane_recv, gtwin_send, gtwin_recv,
@@ -106,7 +110,6 @@
 
     row = lax.broadcasted_iota(jnp.int32, (BLOCK, BLOCK), 0)
     col = lax.broadcasted_iota(jnp.int32, (BLOCK, BLOCK), 1)
-    eye[...] = jnp.where(row == col, 1.0, 0.0).astype(bf16)
     average[...] = jnp.where(row[:128] == col[:128] // 2, 0.5, 0.0).astype(bf16)
     near[OWN, 0] = k_ref[...]
     near[OWN, 1] = v_ref[...]
@@ -166,20 +169,20 @@
             mine = (lane >= 64) if half else (lane < 64)
             qm[2 * pair + half] = jnp.where(mine, queries, 0.0).astype(bf16)
             gm[2 * pair + half] = jnp.where(mine, grads_wide, 0.0).astype(bf16)
-        gt[pair] = dot_nt(eye[:128, :128], grads)
         return carry
 
     lax.fori_loop(0, PAIRS, prepare, 0)
 
-    def forward(load, size, valid, offset, unit, first=False):
+    first_head = lane < 64
+
+    def forward(load, size, valid, offset, unit):
         parts = len(valid)
         step = size // parts
 
         def body(pair, carry):
             lanes = pl.ds(pl.multiple_of(pair * 128, 128), 128)
             keys, values = load(0, lanes), load(1, lanes)
-            kt[lanes, offset : offset + size] = dot_nt(eye[:128, :128], keys).astype(bf16)
-            values_t = dot_nt(eye[:128, :128], values).astype(bf16)
+            outs = []
             for half in range(2):
                 head = 2 * pair + half
                 scores = dot_nt(keys, qm[head])
@@ -190,9 +193,6 @@
                     if flag is not None:
                         peak = jnp.where(flag, peak, -OUTSIDE)
                     high = peak if high is None else jnp.maximum(high, peak)
-                if not first:
-                    before = top[head]
-                    high = jnp.maximum(high, before)
                 weights, sums = [], None
                 for block, flag in zip(blocks, valid):
                     shift = high if flag is None else jnp.where(flag, high, OUTSIDE)
@@ -202,19 +202,13 @@
                     weights.append(weight.astype(bf16))
                 weight = weights[0] if parts == 1 else jnp.concatenate(weights, axis=0)
                 prob[head, offset : offset + size] = weight
-                part = dot_nn(values_t[half * 64 : half * 64 + 64], weight)
-                if first:
-                    total[head] = sums
-                    ot[head] = part
-                else:
-                    fade = jnp.exp(before - high)
-                    total[head] = total[head] * fade + sums
-                    ot[head] = ot[head] * fade + part
-                top[head] = high
-                unit_top[unit, head] = high
+                outs.append(dot_tn(weight, values))
+                top[unit, head] = high
+                total[unit, head] = sums
+            out_part[unit, pair] = jnp.where(first_head, outs[0], outs[1])
             return carry
 
-        lax.fori_loop(0, PAIRS, body, 0)
+        lax.fori_loop(0, PAIRS, body, 0, unroll=True)
 
     def near_load(slot):
         return lambda kv, lanes: near[slot, kv, :, lanes]
@@ -266,7 +260,7 @@
         unit = NEAR_UNITS + level - 1
         forward(piece_load(level), 384, level_valid[level], unit_offset(unit), unit)
 
-    forward(near_load(OWN), BLOCK, [None], unit_offset(0), 0, first=True)
+    forward(near_load(OWN), BLOCK, [None], unit_offset(0), 0)
     arrived(near.at[twin_slot], near_recv.at[twin_slot])
     forward(near_load(twin_slot), BLOCK, [None], unit_offset(1), 1)
     plane_arrived(4)
@@ -289,30 +283,48 @@
     arrived(near.at[far_slot], near_recv.at[far_slot])
     forward(near_load(far_slot), BLOCK, [far_valid], unit_offset(2), 2)
 
+    units = range(NEAR_UNITS + LEVELS)
+    head_row = lax.broadcasted_iota(jnp.int32, (8, 128), 0)
+    head_lane = lax.broadcasted_iota(jnp.int32, (8, 128), 1) // 64
+    head_sum = jnp.where(head_row == head_lane, 1.0, 0.0).astype(bf16)
+
     def finish(pair, carry):
         lanes = pl.ds(pl.multiple_of(pair * 128, 128), 128)
-        outs = []
+        rows = []
         for half in range(2):
             head = 2 * pair + half
-            scale = 1.0 / total[head]
-            out = ot[head] * scale
-            outs.append(out.astype(bf16))
-            delta[head] = jnp.sum(
-                gt[pair, half * 64 : half * 64 + 64] * out, axis=0, keepdims=True
+            high = functools.reduce(jnp.maximum, [top[unit, head] for unit in units])
+            fades = [jnp.exp(top[unit, head] - high) for unit in units]
+            scale = 1.0 / sum(fade * total[unit, head] for unit, fade in zip(units, fades))
+            for unit, fade in zip(units, fades):
+                factor[unit, head] = fade * scale
+                rows.append(fade * scale)
+        rows += [jnp.zeros_like(rows[0])] * (16 - len(rows))
+        columns = jnp.transpose(jnp.concatenate(rows, axis=0))
+        out = None
+        for unit in units:
+            second = len(units) + unit
+            both = jnp.where(
+                first_head, columns[:, unit : unit + 1], columns[:, second : second + 1]
             )
-            high = top[head]
-            for unit in range(NEAR_UNITS + LEVELS):
-                factor[unit, head] = jnp.exp(unit_top[unit, head] - high) * scale
-            dqt[head] = jnp.zeros((HEAD, BLOCK), f32)
-        att_ref[:, lanes] = dot_nt(eye[...], jnp.concatenate(outs, axis=0)).astype(bf16)
+            added = out_part[unit, pair] * both
+            out = added if out is None else out + added
+        att_ref[:, lanes] = out.astype(bf16)
+        product = out * g_ref[:, lanes].astype(f32)
+        coarse = product.astype(bf16)
+        rest = (product - coarse.astype(f32)).astype(bf16)
+        deltas = dot_nt(head_sum, coarse) + dot_nt(head_sum, rest)
+        for half in range(2):
+            delta[2 * pair + half] = deltas[half : half + 1]
+            dq_part[2 * pair + half] = jnp.zeros((BLOCK, 128), f32)
         return carry
 
-    lax.fori_loop(0, PAIRS, finish, 0)
+    lax.fori_loop(0, PAIRS, finish, 0, unroll=True)
 
     def backward(load, size, offset, unit, store):
         def body(pair, carry):
             lanes = pl.ds(pl.multiple_of(pair * 128, 128), 128)
-            values = load(1, lanes)
+            keys, values = load(0, lanes), load(1, lanes)
             key_part, value_part = None, None
             for half in range(2):
                 head = 2 * pair + half
@@ -322,12 +334,11 @@
                 value_new = dot_nn(wide.astype(bf16), gm[head])
                 key_part = key_new if key_part is None else key_part + key_new
                 value_part = value_new if value_part is None else value_part + value_new
-                rows = pl.ds(pl.multiple_of(pair * 128 + half * 64, 64), 64)
-                dqt[head] += dot_nn(kt[rows, offset : offset + size], dscore)
+                dq_part[head] += dot_tn(dscore, keys)
             store(lanes, key_part, value_part)
             return carry
 
-        lax.fori_loop(0, PAIRS, body, 0)
+        lax.fori_loop(0, PAIRS, body, 0, unroll=True)
 
     def near_store(slot):
         def store(lanes, key_part, value_part):
@@ -416,9 +427,8 @@
 
     def write_queries(pair, carry):
         lanes = pl.ds(pl.multiple_of(pair * 128, 128), 128)
-        both = jnp.concatenate([dqt[2 * pair], dqt[2 * pair + 1]], axis=0)
-        both = (both * (1.0 / math.sqrt(HEAD))).astype(bf16)
-        dq_ref[:, lanes] = dot_nt(eye[...], both).astype(bf16)
+        both = jnp.where(first_head, dq_part[2 * pair], dq_part[2 * pair + 1])
+        dq_ref[:, lanes] = (both * (1.0 / math.sqrt(HEAD))).astype(bf16)
         return carry
 
     lax.fori_loop(0, PAIRS, write_queries, 0)
@@ -454,6 +464,23 @@
         copy.wait_send()
 
 
+def hand_over(*refs):
+    sources, targets, (held, in_sem, out_sem) = refs[:4], refs[4:8], refs[8:]
+    inward = [
+        pltpu.make_async_copy(source, held.at[i], in_sem.at[i]) for i, source in enumerate(sources)
+    ]
+    outward = [
+        pltpu.make_async_copy(held.at[i], target, out_sem.at[i]) for i, target in enumerate(targets)
+    ]
+    for copy in inward:
+        copy.start()
+    for first, second in zip(inward, outward):
+        first.wait()
+        second.start()
+    for copy in outward:
+        copy.wait()
+
+
 def on_device(device_count, sub_count, queries, keys, values, cotangent):
     vmem = pl.BlockSpec(memory_space=pltpu.VMEM)
     dma = pltpu.SemaphoreType.DMA
@@ -468,17 +495,13 @@
         pltpu.VMEM((LEVELS, 3, 2, 128, FEATURES), bf16),
         pltpu.VMEM((HEADS, BLOCK, 128), bf16),
         pltpu.VMEM((HEADS, BLOCK, 128), bf16),
-        pltpu.VMEM((PAIRS, 128, BLOCK), f32),
-        pltpu.VMEM((FEATURES, KEYS), bf16),
         pltpu.VMEM((HEADS, KEYS, BLOCK), bf16),
-        pltpu.VMEM((HEADS, 1, BLOCK), f32),
+        pltpu.VMEM((NEAR_UNITS + LEVELS, HEADS, 1, BLOCK), f32),
+        pltpu.VMEM((NEAR_UNITS + LEVELS, HEADS, 1, BLOCK), f32),
+        pltpu.VMEM((NEAR_UNITS + LEVELS, PAIRS, BLOCK, 128), f32),
+        pltpu.VMEM((HEADS, BLOCK, 128), f32),
         pltpu.VMEM((NEAR_UNITS + LEVELS, HEADS, 1, BLOCK), f32),
         pltpu.VMEM((HEADS, 1, BLOCK), f32),
-        pltpu.VMEM((HEADS, HEAD, BLOCK), f32),
-        pltpu.VMEM((HEADS, HEAD, BLOCK), f32),
-        pltpu.VMEM((NEAR_UNITS + LEVELS, HEADS, 1, BLOCK), f32),
-        pltpu.VMEM((HEADS, 1, BLOCK), f32),
-        pltpu.VMEM((BLOCK, BLOCK), bf16),
         pltpu.VMEM((BLOCK, CONTRIBUTIONS), bf16),
         pltpu.VMEM((128, BLOCK), bf16),
         pltpu.VMEM((2, 2) + rows, bf16),
@@ -495,7 +518,7 @@
         dma((plane_messages,)), dma((LEVELS,)),
         dma((3 * LEVELS,)), dma((3 * LEVELS,)),
     ]
-    return pl.pallas_call(
+    results = pl.pallas_call(
         functools.partial(kernel, device_count, sub_count),
         out_shape=[jax.ShapeDtypeStruct(rows, bf16)] * 4,
         in_specs=[vmem] * 4,
@@ -506,6 +529,15 @@
         ),
         name="hierarchical_attention",
     )(queries, keys, values, cotangent)
+    anywhere = pl.BlockSpec(memory_space=pl.ANY)
+    return pl.pallas_call(
+        hand_over,
+        out_shape=[jax.ShapeDtypeStruct(rows, bf16)] * 4,
+        in_specs=[anywhere] * 4,
+        out_specs=[anywhere] * 4,
+        scratch_shapes=[pltpu.VMEM((4,) + rows, bf16), dma((4,)), dma((4,))],
+        name="hand_over",
+    )(*results)
 
 
 def solution(mesh):

time: 99.3 us -> 87.9 us (0.89)
  the two profiles are of different devices: /device:TPU:33 before, /device:TPU:28 now
where the time goes in v1:
time: 87.9 us; the launch traced here: 87.8 us
  Pallas kernels  87 us (99%)
    pallas_call x1, Pallas kernels, on_device(): pl.pallas_call(functools.partial(kernel, device_count, sub_count), out_sh...  85 us
    pallas_call x1, Pallas kernels, on_device(): pl.pallas_call(hand_over, out_shape=[jax.ShapeDtypeStruct(rows, bf16)] *...  1.98 us

profile of v1, /device:TPU:28, one launch (start us, length us, event | category | flops | bytes accessed | tf_op | source)
XLA Modules:
  0.0 87.8 jit_solution(9300545965351314466)
XLA Ops:
  0.6 85.0 %hierarchical_attention.1 = (bf16[256,512]{1,0:T(8,128)(2,1)}, bf16[256,512]{1,0:T(8,128)(2,1)}, bf16[256,512]{1,0:T(8,128)(2,1)}, bf16[256,512]{1,0:T(8,128)(2,1)}) custom-call(bf16[256,512]{1,0:T(8,128)(2,1)} %q_ref.1, bf16[256,512]{1,0:T(8,128)(2,1)} %k_ref.1, bf16[256,512]{1,0:T(8,128)(2,1)} %v_ref.1, bf16[256,512]{1,0:T(8,128)(2,1)} %g_ref.1), custom_call_target="tpu_custom_call" | custom-call | tf_op jit(solution)/shard_map/hierarchical_attention/pallas_call | solution.py:521
  85.6 2.0 %hand_over.1 = (bf16[256,512]{1,0:T(8,128)(2,1)}, bf16[256,512]{1,0:T(8,128)(2,1)}, bf16[256,512]{1,0:T(8,128)(2,1)}, bf16[256,512]{1,0:T(8,128)(2,1)}) custom-call(bf16[256,512]{1,0:T(8,128)(2,1)} %get-tuple-element.8.refs_0_, bf16[256,512]{1,0:T(8,128)(2,1)} %get-tuple-element.9.refs_1_, bf16[256,512]{1,0:T(8,128)(2,1)} %get-tuple-element.10.refs_2_, ...), custom_call_target="tpu_custom_call" | custom-call | tf_op jit(solution)/shard_map/hand_over/pallas_call | solution.py:533

commit v2 on v1

v2 whole, which is shorter than its diff:
```python
import functools
import math

import jax
import jax.numpy as jnp
from jax import lax
from jax.experimental import pallas as pl
from jax.experimental.pallas import tpu as pltpu
from jax.sharding import PartitionSpec as P

MESH = pl.DeviceIdType.MESH
HEADS = 8
HEAD = 64
BLOCK = 256
FEATURES = 512
LEVELS = 4
PAIRS = HEADS // 2
NEAR_UNITS = 3
KEYS = 3 * BLOCK + 3 * LEVELS * 128
CONTRIBUTIONS = 128 + 2 * 192 + 64
OUTSIDE = 1e30
bf16 = jnp.bfloat16
f32 = jnp.float32

OWN, LEFT, RIGHT = 0, 1, 2


def dot_nt(a, b):
    return lax.dot_general(a, b, (((1,), (1,)), ((), ())), preferred_element_type=f32)


def dot_tn(a, b):
    return lax.dot_general(a, b, (((0,), (0,)), ((), ())), preferred_element_type=f32)


def dot_nn(a, b):
    return lax.dot_general(a, b, (((1,), (0,)), ((), ())), preferred_element_type=f32)


def level_rows(level):
    return BLOCK >> level


def unit_offset(unit):
    return unit * BLOCK if unit < NEAR_UNITS else 3 * BLOCK + (unit - NEAR_UNITS) * 384


def contribution_base(level):
    return (0, 128, 320, 512)[level - 1]


def contribution_width(level):
    return (128, 192, 192, 64)[level - 1]


def kernel(
    device_count,
    sub_count,
    q_ref, k_ref, v_ref, g_ref,
    att_ref, dq_ref, dk_ref, dv_ref,
    near, lev1, lev2, lev3, lev4, pieces,
    qm, gm, prob, top, total, out_part, dq_part, factor, delta,
    upsample, average,
    near_grad, own_grad, piece_grad, twin_grad, twin_first, near_in, coarse_in,
    row_keys, row_grads, row_sum, derived,
    near_send, near_recv, plane_send, plane_recv, twin_send, twin_recv,
    gnear_send, gnear_recv, gplane_send, gplane_recv, gtwin_send, gtwin_recv,
    row_send, row_recv, grow_send, grow_recv,
):
    n = device_count
    me = lax.axis_index("seq") * sub_count + lax.axis_index("sub")
    core = lax.rem(me, 2)
    twin = me + 1 - 2 * core
    levels = [lev1, lev2, lev3, lev4]

    def wrapped(device):
        return lax.rem(device + n, n)

    def mesh_id(device):
        return (device // sub_count, lax.rem(device, sub_count))

    def group_size(level):
        return 2 ** (level - 1)

    def chips(level):
        return max(group_size(level) // 2, 1)

    def chip_place(level):
        return lax.rem(me // 2, chips(level))

    def group_targets(level):
        size = group_size(level)
        group = me // size
        count = n // size
        odd = lax.rem(group, 2)
        third = lax.rem(group + 3 - 6 * odd + count, count)
        below = lax.rem(group - 2 + count, count)
        above = lax.rem(group + 2, count)
        return [below * size, above * size, third * size]

    row_place = lax.rem(me // 2, 4)
    row_start = me - lax.rem(me, 8)

    def plane_chips(level):
        return 1 if level == 4 else chips(level)

    def plane_target(level, start, chip):
        if level == 1:
            return start
        if level == 4:
            return start + lax.rem(me, 8)
        return start + 2 * chip + core

    def row_partner(step):
        place = lax.rem(row_place + step, 4)
        return place, row_start + 2 * place + core

    partners = [twin, wrapped(me - 1 + 2 * core)]
    for level in range(1, LEVELS + 1):
        starts = group_targets(level)[: 2 if level == 1 else 3]
        for start in starts:
            for chip in range(plane_chips(level)):
                partners.append(plane_target(level, start, chip))
    partners += [row_partner(step)[1] for step in (1, 2, 3)]

    barrier = pltpu.get_barrier_semaphore()
    for partner in partners:
        pl.semaphore_signal(barrier, inc=1, device_id=mesh_id(partner), device_id_type=MESH)

    row = lax.broadcasted_iota(jnp.int32, (BLOCK, BLOCK), 0)
    col = lax.broadcasted_iota(jnp.int32, (BLOCK, BLOCK), 1)
    average[...] = jnp.where(row[:128] == col[:128] // 2, 0.5, 0.0).astype(bf16)
    near[OWN, 0] = k_ref[...]
    near[OWN, 1] = v_ref[...]
    for kv in range(2):
        lev1[kv] = dot_nn(average[...], near[OWN, kv]).astype(bf16)
    for level in range(2, LEVELS + 1):
        fine, coarse = levels[level - 2], levels[level - 1]
        rows = level_rows(level)
        for kv in range(2):
            coarse[kv] = dot_nn(average[:rows, : 2 * rows], fine[kv]).astype(bf16)
    own_row = pl.ds(pl.multiple_of(row_place * 16, 16), 16)
    for kv in range(2):
        row_keys[kv, own_row] = lev4[kv]

    pl.semaphore_wait(barrier, len(partners))

    started = []

    def remote(src, dst, send, recv, device):
        copy = pltpu.make_async_remote_copy(
            src_ref=src, dst_ref=dst, send_sem=send, recv_sem=recv,
            device_id=mesh_id(device), device_id_type=MESH,
        )
        copy.start()
        started.append(copy)

    def arrived(ref, sem):
        pltpu.make_async_copy(ref, ref, sem).wait()

    def group_lanes(part):
        return pl.ds(part * 256, 256)

    for step in (1, 3, 2):
        remote(
            lev4, row_keys.at[:, own_row], row_send.at[step - 1], row_recv.at[step - 1],
            row_partner(step)[1],
        )
    far_slot = LEFT + core
    twin_slot = RIGHT - core
    far_device = wrapped(me - 1 + 2 * core)
    half_rows = pl.ds(pl.multiple_of(core * 64, 64), 64)
    other_rows = pl.ds(pl.multiple_of(64 - core * 64, 64), 64)

    def send_keys(part):
        lanes = group_lanes(part)
        block = near.at[OWN, :, :, lanes]
        remote(
            block, near.at[RIGHT - core, :, :, lanes],
            near_send.at[part, 0], near_recv.at[part, 0], far_device,
        )
        remote(
            block, near.at[LEFT + core, :, :, lanes],
            near_send.at[part, 1], near_recv.at[part, 1], twin,
        )
        place = 0
        for level in (3, 2):
            rows = level_rows(level)
            targets = group_targets(level)
            for slot, start in ((1, targets[0]), (0, targets[1]), (2, targets[2])):
                for chip in range(chips(level)):
                    offset = pl.multiple_of(core * 64 + chip_place(level) * rows, 16)
                    remote(
                        levels[level - 1].at[:, :, lanes],
                        pieces.at[level - 1, slot, :, pl.ds(offset, rows), lanes],
                        plane_send.at[part, place],
                        plane_recv.at[part, 3 * (level - 1) + slot],
                        plane_target(level, start, chip),
                    )
                    place += 1
        remote(
            lev1.at[:, :, lanes], pieces.at[0, core, :, :, lanes],
            plane_send.at[part, place], plane_recv.at[part, 0], wrapped(me + 2 - 4 * core),
        )

    def send_row(part):
        lanes = group_lanes(part)
        targets = group_targets(4)
        for slot, start in ((1, targets[0]), (0, targets[1]), (2, targets[2])):
            remote(
                row_keys.at[:, :, lanes], pieces.at[3, slot, :, half_rows, lanes],
                plane_send.at[part, 10 + slot], plane_recv.at[part, 9 + slot],
                plane_target(4, start, 0),
            )

    send_keys(0)
    for step in (1, 3, 2):
        from_place = lax.rem(row_place + 4 - step, 4)
        arrived(
            row_keys.at[:, pl.ds(pl.multiple_of(from_place * 16, 16), 16)], row_recv.at[step - 1]
        )
    send_row(0)
    send_keys(1)
    send_row(1)

    lane = lax.broadcasted_iota(jnp.int32, (BLOCK, 128), 1)
    first_head = lane < 64

    def pairs_of(part):
        return range(2 * part, 2 * part + 2)

    def pair_lanes(pair):
        return slice(pair * 128, pair * 128 + 128)

    for pair in range(PAIRS):
        lanes = pair_lanes(pair)
        queries = q_ref[:, lanes].astype(f32) * (1.0 / math.sqrt(HEAD))
        grads = g_ref[:, lanes].astype(f32)
        for half in range(2):
            mine = (lane >= 64) if half else (lane < 64)
            qm[2 * pair + half] = jnp.where(mine, queries, 0.0).astype(bf16)
            gm[2 * pair + half] = jnp.where(mine, grads, 0.0).astype(bf16)

    for level in range(1, LEVELS + 1):
        count = level_rows(level)
        base = contribution_base(level)
        width = contribution_width(level)
        r = lax.broadcasted_iota(jnp.int32, (BLOCK, width), 0)
        c = lax.broadcasted_iota(jnp.int32, (BLOCK, width), 1)
        upsample[:, base : base + width] = jnp.where(
            lax.rem(c, count) == r // 2**level, 0.5**level, 0.0
        ).astype(bf16)

    def forward(part, load, size, valid, offset, unit):
        blocks_in = len(valid)
        step = size // blocks_in
        for pair in pairs_of(part):
            lanes = pair_lanes(pair)
            keys, values = load(0, lanes), load(1, lanes)
            outs = []
            for half in range(2):
                head = 2 * pair + half
                scores = dot_nt(keys, qm[head])
                blocks = [scores[i * step : (i + 1) * step] for i in range(blocks_in)]
                high = None
                for block, flag in zip(blocks, valid):
                    peak = jnp.max(block, axis=0, keepdims=True)
                    if flag is not None:
                        peak = jnp.where(flag, peak, -OUTSIDE)
                    high = peak if high is None else jnp.maximum(high, peak)
                weights, sums = [], None
                for block, flag in zip(blocks, valid):
                    shift = high if flag is None else jnp.where(flag, high, OUTSIDE)
                    weight = jnp.exp(block - shift)
                    added = jnp.sum(weight, axis=0, keepdims=True)
                    sums = added if sums is None else sums + added
                    weights.append(weight.astype(bf16))
                weight = weights[0] if blocks_in == 1 else jnp.concatenate(weights, axis=0)
                prob[head, offset : offset + size] = weight
                outs.append(dot_tn(weight, values))
                top[unit, head] = high
                total[unit, head] = sums
            out_part[unit, pair] = jnp.where(first_head, outs[0], outs[1])

    def near_load(slot):
        return lambda kv, lanes: near[slot, kv, :, lanes]

    def piece_load(level):
        return lambda kv, lanes: jnp.concatenate(
            [pieces[level - 1, slot, kv, :, lanes] for slot in range(3)], axis=0
        )

    far_valid = jnp.logical_or(
        jnp.logical_and(core == 0, me >= 1), jnp.logical_and(core == 1, me < n - 1)
    )
    level_valid = {}
    for level in range(1, LEVELS + 1):
        size = group_size(level)
        group, count = me // size, n // size
        odd = lax.rem(group, 2)
        third = group + 3 - 6 * odd
        level_valid[level] = [
            group >= 2,
            group + 2 < count,
            jnp.logical_and(third >= 0, third < count),
        ]

    def pass_on(part, level):
        lanes = group_lanes(part)
        for slot in range(3):
            at = 3 * (level - 1) + slot
            ref = pieces.at[level - 1, slot, :, half_rows, lanes]
            arrived(ref, plane_recv.at[part, at])
            remote(ref, ref, twin_send.at[part, at], twin_recv.at[part, at], twin)

    def pass_on_first(part):
        lanes = group_lanes(part)
        ref = pieces.at[0, core, :, :, lanes]
        arrived(ref, plane_recv.at[part, 0])
        remote(
            ref, pieces.at[0, 2, :, :, lanes],
            twin_send.at[part, 0], twin_recv.at[part, 0], twin,
        )

    def forward_level(part, level):
        lanes = group_lanes(part)
        if level == 1:
            arrived(pieces.at[0, 2, :, :, lanes], twin_recv.at[part, 0])
            arrived(pieces.at[0, 1 - core, :, :, lanes], twin_recv.at[part, 1])
        else:
            for slot in range(3):
                arrived(
                    pieces.at[level - 1, slot, :, other_rows, lanes],
                    twin_recv.at[part, 3 * (level - 1) + slot],
                )
        unit = NEAR_UNITS + level - 1
        forward(part, piece_load(level), 384, level_valid[level], unit_offset(unit), unit)

    def forward_own(part):
        forward(part, near_load(OWN), BLOCK, [None], unit_offset(0), 0)

    def forward_twin(part):
        arrived(near.at[twin_slot, :, :, group_lanes(part)], near_recv.at[part, 1])
        forward(part, near_load(twin_slot), BLOCK, [None], unit_offset(1), 1)

    def forward_far(part):
        lanes = group_lanes(part)
        arrived(near.at[far_slot, :, :, lanes], near_recv.at[part, 0])
        for kv in range(2):
            derived[kv, :, lanes] = dot_nn(average[...], near[far_slot, kv, :, lanes]).astype(bf16)
        remote(
            derived.at[:, :, lanes], pieces.at[0, core, :, :, lanes],
            twin_send.at[part, 1], twin_recv.at[part, 1], twin,
        )
        forward(part, near_load(far_slot), BLOCK, [far_valid], unit_offset(2), 2)

    units = range(NEAR_UNITS + LEVELS)
    head_row = lax.broadcasted_iota(jnp.int32, (8, 128), 0)
    head_lane = lax.broadcasted_iota(jnp.int32, (8, 128), 1) // 64
    head_sum = jnp.where(head_row == head_lane, 1.0, 0.0).astype(bf16)

    def finish(part):
        for pair in pairs_of(part):
            lanes = pair_lanes(pair)
            rows = []
            for half in range(2):
                head = 2 * pair + half
                high = functools.reduce(jnp.maximum, [top[unit, head] for unit in units])
                fades = [jnp.exp(top[unit, head] - high) for unit in units]
                scale = 1.0 / sum(fade * total[unit, head] for unit, fade in zip(units, fades))
                for unit, fade in zip(units, fades):
                    factor[unit, head] = fade * scale
                    rows.append(fade * scale)
            rows += [jnp.zeros_like(rows[0])] * (16 - len(rows))
            columns = jnp.transpose(jnp.concatenate(rows, axis=0))
            out = None
            for unit in units:
                second = len(units) + unit
                both = jnp.where(
                    first_head, columns[:, unit : unit + 1], columns[:, second : second + 1]
                )
                added = out_part[unit, pair] * both
                out = added if out is None else out + added
            att_ref[:, lanes] = out.astype(bf16)
            product = out * g_ref[:, lanes].astype(f32)
            coarse = product.astype(bf16)
            rest = (product - coarse.astype(f32)).astype(bf16)
            deltas = dot_nt(head_sum, coarse) + dot_nt(head_sum, rest)
            for half in range(2):
                delta[2 * pair + half] = deltas[half : half + 1]
                dq_part[2 * pair + half] = jnp.zeros((BLOCK, 128), f32)

    def backward(part, load, size, offset, unit, store):
        for pair in pairs_of(part):
            lanes = pair_lanes(pair)
            keys, values = load(0, lanes), load(1, lanes)
            key_part, value_part = None, None
            for half in range(2):
                head = 2 * pair + half
                wide = prob[head, offset : offset + size].astype(f32) * factor[unit, head]
                dscore = (wide * (dot_nt(values, gm[head]) - delta[head])).astype(bf16)
                key_new = dot_nn(dscore, qm[head])
                value_new = dot_nn(wide.astype(bf16), gm[head])
                key_part = key_new if key_part is None else key_part + key_new
                value_part = value_new if value_part is None else value_part + value_new
                dq_part[head] += dot_tn(dscore, keys)
            store(lanes, key_part, value_part)

    def near_store(slot):
        def store(lanes, key_part, value_part):
            near_grad[slot, 0, :, lanes] = key_part.astype(bf16)
            near_grad[slot, 1, :, lanes] = value_part.astype(bf16)
        return store

    def own_store(lanes, key_part, value_part):
        own_grad[0, :, lanes] = key_part
        own_grad[1, :, lanes] = value_part

    def piece_store(level):
        def store(lanes, key_part, value_part):
            for slot in range(3):
                at = slice(slot * 128, slot * 128 + 128)
                piece_grad[level - 1, slot, 0, :, lanes] = key_part[at].astype(bf16)
                piece_grad[level - 1, slot, 1, :, lanes] = value_part[at].astype(bf16)
        return store

    def backward_level(part, level):
        unit = NEAR_UNITS + level - 1
        backward(part, piece_load(level), 384, unit_offset(unit), unit, piece_store(level))
        lanes = group_lanes(part)
        if level == 1:
            for i, slot in enumerate((2, 1 - core)):
                remote(
                    piece_grad.at[0, slot, :, :, lanes], twin_first.at[i, :, :, lanes],
                    gtwin_send.at[part, i], gtwin_recv.at[part, i], twin,
                )
            return
        for slot in range(3):
            at = 3 * (level - 1) + slot
            remote(
                piece_grad.at[level - 1, slot, :, other_rows, lanes],
                twin_grad.at[level - 2, slot, :, :, lanes],
                gtwin_send.at[part, at], gtwin_recv.at[part, at], twin,
            )

    def grads_to_owners(part, level):
        lanes = group_lanes(part)
        rows = level_rows(level)
        for slot in range(3):
            arrived(
                twin_grad.at[level - 2, slot, :, :, lanes],
                gtwin_recv.at[part, 3 * (level - 1) + slot],
            )
            for kv in range(2):
                piece_grad[level - 1, slot, kv, half_rows, lanes] = (
                    piece_grad[level - 1, slot, kv, half_rows, lanes].astype(f32)
                    + twin_grad[level - 2, slot, kv, :, lanes].astype(f32)
                ).astype(bf16)
        targets = group_targets(level)
        place = {4: 1, 3: 4, 2: 10}[level]
        for slot in range(3):
            for chip in range(plane_chips(level)):
                if level == 4:
                    remote(
                        piece_grad.at[3, slot, :, half_rows, lanes],
                        row_grads.at[slot, :, :, lanes],
                        gplane_send.at[part, place], gplane_recv.at[part, 3 + slot],
                        plane_target(4, targets[slot], 0),
                    )
                else:
                    source = pl.multiple_of(core * 64 + chip * rows, 16)
                    base = contribution_base(level) + slot * 64
                    target = pl.multiple_of(base + chip_place(level) * rows, 16)
                    remote(
                        piece_grad.at[level - 1, slot, :, pl.ds(source, rows), lanes],
                        coarse_in.at[:, pl.ds(target, rows), lanes],
                        gplane_send.at[part, place], gplane_recv.at[part, level - 1],
                        plane_target(level, targets[slot], chip),
                    )
                place += 1

    def first_to_owner(part):
        lanes = group_lanes(part)
        arrived(twin_first.at[0, :, :, lanes], gtwin_recv.at[part, 0])
        for kv in range(2):
            piece_grad[0, core, kv, :, lanes] = (
                piece_grad[0, core, kv, :, lanes].astype(f32)
                + twin_first[0, kv, :, lanes].astype(f32)
            ).astype(bf16)
        remote(
            piece_grad.at[0, core, :, :, lanes], coarse_in.at[:, pl.ds(0, 128), lanes],
            gplane_send.at[part, 0], gplane_recv.at[part, 0], wrapped(me - 2 + 4 * core),
        )

    def backward_far(part):
        lanes = group_lanes(part)
        backward(part, near_load(far_slot), BLOCK, unit_offset(2), 2, near_store(1))
        arrived(twin_first.at[1, :, :, lanes], gtwin_recv.at[part, 1])
        for kv in range(2):
            near_grad[1, kv, :, lanes] = (
                near_grad[1, kv, :, lanes].astype(f32)
                + dot_nn(upsample[:, :128], twin_first[1, kv, :, lanes])
            ).astype(bf16)
        remote(
            near_grad.at[1, :, :, lanes], near_in.at[1, :, :, lanes],
            gnear_send.at[part, 1], gnear_recv.at[part, 1], far_device,
        )

    def backward_twin(part):
        lanes = group_lanes(part)
        backward(part, near_load(twin_slot), BLOCK, unit_offset(1), 1, near_store(0))
        remote(
            near_grad.at[0, :, :, lanes], near_in.at[0, :, :, lanes],
            gnear_send.at[part, 0], gnear_recv.at[part, 0], twin,
        )

    def backward_own(part):
        backward(part, near_load(OWN), BLOCK, unit_offset(0), 0, own_store)
        for pair in pairs_of(part):
            both = jnp.where(first_head, dq_part[2 * pair], dq_part[2 * pair + 1])
            dq_ref[:, pair_lanes(pair)] = (both * (1.0 / math.sqrt(HEAD))).astype(bf16)

    def row_to_owners(part):
        lanes = group_lanes(part)
        for slot in range(3):
            arrived(row_grads.at[slot, :, :, lanes], gplane_recv.at[part, 3 + slot])
        for kv in range(2):
            added = row_grads[0, kv, :, lanes].astype(f32) + row_grads[1, kv, :, lanes].astype(f32)
            row_sum[kv, :, lanes] = (added + row_grads[2, kv, :, lanes].astype(f32)).astype(bf16)
        target = pl.ds(pl.multiple_of(contribution_base(4) + row_place * 16, 16), 16)
        for kv in range(2):
            coarse_in[kv, target, lanes] = row_sum[kv, own_row, lanes]
        for step in (1, 3, 2):
            place, device = row_partner(step)
            remote(
                row_sum.at[:, pl.ds(pl.multiple_of(place * 16, 16), 16), lanes],
                coarse_in.at[:, target, lanes],
                grow_send.at[part, step - 1], grow_recv.at[part, step - 1], device,
            )

    def write(part):
        lanes = group_lanes(part)
        arrived(near_in.at[0, :, :, lanes], gnear_recv.at[part, 0])
        arrived(near_in.at[1, :, :, lanes], gnear_recv.at[part, 1])
        for level in range(1, LEVELS):
            base, width = contribution_base(level), contribution_width(level)
            arrived(coarse_in.at[:, pl.ds(base, width), lanes], gplane_recv.at[part, level - 1])
        for step in (1, 3, 2):
            base = contribution_base(4) + lax.rem(row_place + 4 - step, 4) * 16
            arrived(
                coarse_in.at[:, pl.ds(pl.multiple_of(base, 16), 16), lanes],
                grow_recv.at[part, step - 1],
            )
        for kv, out_ref in ((0, dk_ref), (1, dv_ref)):
            out = own_grad[kv, :, lanes] + near_in[0, kv, :, lanes].astype(f32)
            out = out + near_in[1, kv, :, lanes].astype(f32)
            out = out + dot_nn(upsample[...], coarse_in[kv, :, lanes])
            out_ref[:, lanes] = out.astype(bf16)

    forward_own(0)
    forward_own(1)
    forward_twin(0)
    pass_on(0, 3)
    pass_on(0, 2)
    forward_level(0, 3)
    pass_on(0, 4)
    pass_on_first(0)
    forward_level(0, 2)
    forward_far(0)
    forward_level(0, 4)
    forward_twin(1)
    forward_level(0, 1)
    finish(0)
    backward_level(0, 1)
    backward_level(0, 4)
    first_to_owner(0)
    backward_far(0)
    grads_to_owners(0, 4)
    pass_on(1, 3)
    backward_level(0, 3)
    pass_on(1, 2)
    backward_level(0, 2)
    grads_to_owners(0, 3)
    pass_on(1, 4)
    pass_on_first(1)
    backward_twin(0)
    grads_to_owners(0, 2)
    forward_level(1, 3)
    forward_level(1, 2)
    forward_level(1, 4)
    forward_far(1)
    backward_own(0)
    row_to_owners(0)
    forward_level(1, 1)
    finish(1)
    backward_level(1, 1)
    backward_level(1, 4)
    first_to_owner(1)
    backward_far(1)
    grads_to_owners(1, 4)
    backward_level(1, 3)
    backward_level(1, 2)
    grads_to_owners(1, 3)
    backward_twin(1)
    grads_to_owners(1, 2)
    backward_own(1)
    write(0)
    row_to_owners(1)
    write(1)
    for copy in started:
        copy.wait_send()


def hand_over(*refs):
    sources, targets, (held, in_sem, out_sem) = refs[:4], refs[4:8], refs[8:]
    inward = [
        pltpu.make_async_copy(source, held.at[i], in_sem.at[i]) for i, source in enumerate(sources)
    ]
    outward = [
        pltpu.make_async_copy(held.at[i], target, out_sem.at[i]) for i, target in enumerate(targets)
    ]
    for copy in inward:
        copy.start()
    for first, second in zip(inward, outward):
        first.wait()
        second.start()
    for copy in outward:
        copy.wait()


def on_device(device_count, sub_count, queries, keys, values, cotangent):
    vmem = pl.BlockSpec(memory_space=pltpu.VMEM)
    dma = pltpu.SemaphoreType.DMA
    rows = (BLOCK, FEATURES)
    plane_messages = 1 + 3 + 6 + 3
    scratch = [
        pltpu.VMEM((3, 2) + rows, bf16),
        pltpu.VMEM((2, 128, FEATURES), bf16),
        pltpu.VMEM((2, 64, FEATURES), bf16),
        pltpu.VMEM((2, 32, FEATURES), bf16),
        pltpu.VMEM((2, 16, FEATURES), bf16),
        pltpu.VMEM((LEVELS, 3, 2, 128, FEATURES), bf16),
        pltpu.VMEM((HEADS, BLOCK, 128), bf16),
        pltpu.VMEM((HEADS, BLOCK, 128), bf16),
        pltpu.VMEM((HEADS, KEYS, BLOCK), bf16),
        pltpu.VMEM((NEAR_UNITS + LEVELS, HEADS, 1, BLOCK), f32),
        pltpu.VMEM((NEAR_UNITS + LEVELS, HEADS, 1, BLOCK), f32),
        pltpu.VMEM((NEAR_UNITS + LEVELS, PAIRS, BLOCK, 128), f32),
        pltpu.VMEM((HEADS, BLOCK, 128), f32),
        pltpu.VMEM((NEAR_UNITS + LEVELS, HEADS, 1, BLOCK), f32),
        pltpu.VMEM((HEADS, 1, BLOCK), f32),
        pltpu.VMEM((BLOCK, CONTRIBUTIONS), bf16),
        pltpu.VMEM((128, BLOCK), bf16),
        pltpu.VMEM((2, 2) + rows, bf16),
        pltpu.VMEM((2,) + rows, f32),
        pltpu.VMEM((LEVELS, 3, 2, 128, FEATURES), bf16),
        pltpu.VMEM((LEVELS - 1, 3, 2, 64, FEATURES), bf16),
        pltpu.VMEM((2, 2, 128, FEATURES), bf16),
        pltpu.VMEM((2, 2) + rows, bf16),
        pltpu.VMEM((2, CONTRIBUTIONS, FEATURES), bf16),
        pltpu.VMEM((2, 64, FEATURES), bf16),
        pltpu.VMEM((3, 2, 64, FEATURES), bf16),
        pltpu.VMEM((2, 64, FEATURES), bf16),
        pltpu.VMEM((2, 128, FEATURES), bf16),
        dma((2, 2)), dma((2, 2)),
        dma((2, plane_messages)), dma((2, 3 * LEVELS)),
        dma((2, 3 * LEVELS)), dma((2, 3 * LEVELS)),
        dma((2, 2)), dma((2, 2)),
        dma((2, plane_messages)), dma((2, LEVELS + 2)),
        dma((2, 3 * LEVELS)), dma((2, 3 * LEVELS)),
        dma((3,)), dma((3,)), dma((2, 3)), dma((2, 3)),
    ]
    results = pl.pallas_call(
        functools.partial(kernel, device_count, sub_count),
        out_shape=[jax.ShapeDtypeStruct(rows, bf16)] * 4,
        in_specs=[vmem] * 4,
        out_specs=[vmem] * 4,
        scratch_shapes=scratch,
        compiler_params=pltpu.CompilerParams(
            collective_id=0, has_side_effects=True, vmem_limit_bytes=56 * 2**20
        ),
        name="hierarchical_attention",
    )(queries, keys, values, cotangent)
    anywhere = pl.BlockSpec(memory_space=pl.ANY)
    return pl.pallas_call(
        hand_over,
        out_shape=[jax.ShapeDtypeStruct(rows, bf16)] * 4,
        in_specs=[anywhere] * 4,
        out_specs=[anywhere] * 4,
        scratch_shapes=[pltpu.VMEM((4,) + rows, bf16), dma((4,)), dma((4,))],
        name="hand_over",
    )(*results)


def solution(mesh):
    spec = P(("seq", "sub"), None)
    device_count = mesh.shape["seq"] * mesh.shape["sub"]
    return jax.shard_map(
        functools.partial(on_device, device_count, mesh.shape["sub"]),
        mesh=mesh,
        in_specs=(spec,) * 4,
        out_specs=(spec,) * 4,
        check_vma=False,
    )
```

time: 87.9 us -> 79.4 us (0.903)
  the two profiles are of different devices: /device:TPU:28 before, /device:TPU:3 now
where the time goes in v2:
time: 79.4 us; the launch traced here: 79.3 us
  Pallas kernels  78.5 us (99%)
  between operations  0.82 us (1%)
    pallas_call x1, Pallas kernels, on_device(): pl.pallas_call(functools.partial(kernel, device_count, sub_count), out_sh...  76.5 us
    pallas_call x1, Pallas kernels, on_device(): pl.pallas_call(hand_over, out_shape=[jax.ShapeDtypeStruct(rows, bf16)] *...  1.98 us

profile of v2, /device:TPU:3, one launch (start us, length us, event | category | flops | bytes accessed | tf_op | source)
XLA Modules:
  0.0 79.3 jit_solution(11453565740604087073)
XLA Ops:
  0.6 76.5 %hierarchical_attention.1 = (bf16[256,512]{1,0:T(8,128)(2,1)}, bf16[256,512]{1,0:T(8,128)(2,1)}, bf16[256,512]{1,0:T(8,128)(2,1)}, bf16[256,512]{1,0:T(8,128)(2,1)}) custom-call(bf16[256,512]{1,0:T(8,128)(2,1)} %q_ref.1, bf16[256,512]{1,0:T(8,128)(2,1)} %k_ref.1, bf16[256,512]{1,0:T(8,128)(2,1)} %v_ref.1, bf16[256,512]{1,0:T(8,128)(2,1)} %g_ref.1), custom_call_target="tpu_custom_call" | custom-call | tf_op jit(solution)/shard_map/hierarchical_attention/pallas_call | solution.py:673
  77.1 2.0 %hand_over.1 = (bf16[256,512]{1,0:T(8,128)(2,1)}, bf16[256,512]{1,0:T(8,128)(2,1)}, bf16[256,512]{1,0:T(8,128)(2,1)}, bf16[256,512]{1,0:T(8,128)(2,1)}) custom-call(bf16[256,512]{1,0:T(8,128)(2,1)} %get-tuple-element.8.refs_0_, bf16[256,512]{1,0:T(8,128)(2,1)} %get-tuple-element.9.refs_1_, bf16[256,512]{1,0:T(8,128)(2,1)} %get-tuple-element.10.refs_2_, ...), custom_call_target="tpu_custom_call" | custom-call | tf_op jit(solution)/shard_map/hand_over/pallas_call | solution.py:685

commit v3 on v2

--- a/solution.py
+++ b/solution.py
@@ -17,7 +17,7 @@
 PAIRS = HEADS // 2
 NEAR_UNITS = 3
 KEYS = 3 * BLOCK + 3 * LEVELS * 128
-CONTRIBUTIONS = 128 + 2 * 192 + 64
+CONTRIBUTIONS = 128 + 128 + 192 + 64
 OUTSIDE = 1e30
 bf16 = jnp.bfloat16
 f32 = jnp.float32
@@ -46,11 +46,11 @@
 
 
 def contribution_base(level):
-    return (0, 128, 320, 512)[level - 1]
+    return (0, 128, 256, 448)[level - 1]
 
 
 def contribution_width(level):
-    return (128, 192, 192, 64)[level - 1]
+    return (128, 128, 192, 64)[level - 1]
 
 
 def kernel(
@@ -62,7 +62,7 @@
     qm, gm, prob, top, total, out_part, dq_part, factor, delta,
     upsample, average,
     near_grad, own_grad, piece_grad, twin_grad, twin_first, near_in, coarse_in,
-    row_keys, row_grads, row_sum, derived,
+    row_keys, row_grads, row_sum, derived, relayed,
     near_send, near_recv, plane_send, plane_recv, twin_send, twin_recv,
     gnear_send, gnear_recv, gplane_send, gplane_recv, gtwin_send, gtwin_recv,
     row_send, row_recv, grow_send, grow_recv,
@@ -172,6 +172,11 @@
     half_rows = pl.ds(pl.multiple_of(core * 64, 64), 64)
     other_rows = pl.ds(pl.multiple_of(64 - core * 64, 64), 64)
 
+    chip_odd = lax.rem(me // 2, 2)
+    beside = wrapped(me + 2 - 4 * chip_odd)
+    two_off = wrapped(me - 4 + 8 * chip_odd)
+    two_back = wrapped(me + 4 - 8 * chip_odd)
+
     def send_keys(part):
         lanes = group_lanes(part)
         block = near.at[OWN, :, :, lanes]
@@ -184,20 +189,27 @@
             near_send.at[part, 1], near_recv.at[part, 1], twin,
         )
         place = 0
-        for level in (3, 2):
-            rows = level_rows(level)
-            targets = group_targets(level)
-            for slot, start in ((1, targets[0]), (0, targets[1]), (2, targets[2])):
-                for chip in range(chips(level)):
-                    offset = pl.multiple_of(core * 64 + chip_place(level) * rows, 16)
-                    remote(
-                        levels[level - 1].at[:, :, lanes],
-                        pieces.at[level - 1, slot, :, pl.ds(offset, rows), lanes],
-                        plane_send.at[part, place],
-                        plane_recv.at[part, 3 * (level - 1) + slot],
-                        plane_target(level, start, chip),
-                    )
-                    place += 1
+        rows = level_rows(2)
+        offset = pl.multiple_of(core * 64, 64)
+        third = group_targets(2)[2] + core
+        for slot, device in ((2, third), (1 - chip_odd, two_off)):
+            remote(
+                lev2.at[:, :, lanes], pieces.at[1, slot, :, pl.ds(offset, rows), lanes],
+                plane_send.at[part, place], plane_recv.at[part, 3 + slot], device,
+            )
+            place += 1
+        rows = level_rows(3)
+        targets = group_targets(3)
+        for slot, start in ((1, targets[0]), (0, targets[1]), (2, targets[2])):
+            for chip in range(chips(3)):
+                offset = pl.multiple_of(core * 64 + chip_place(3) * rows, 16)
+                remote(
+                    lev3.at[:, :, lanes],
+                    pieces.at[2, slot, :, pl.ds(offset, rows), lanes],
+                    plane_send.at[part, place], plane_recv.at[part, 6 + slot],
+                    plane_target(3, start, chip),
+                )
+                place += 1
         remote(
             lev1.at[:, :, lanes], pieces.at[0, core, :, :, lanes],
             plane_send.at[part, place], plane_recv.at[part, 0], wrapped(me + 2 - 4 * core),
@@ -220,8 +232,8 @@
             row_keys.at[:, pl.ds(pl.multiple_of(from_place * 16, 16), 16)], row_recv.at[step - 1]
         )
     send_row(0)
+    send_row(1)
     send_keys(1)
-    send_row(1)
 
     lane = lax.broadcasted_iota(jnp.int32, (BLOCK, 128), 1)
     first_head = lane < 64
@@ -307,10 +319,15 @@
 
     def pass_on(part, level):
         lanes = group_lanes(part)
-        for slot in range(3):
+        for slot in (2, 1 - chip_odd, chip_odd) if level == 2 else range(3):
             at = 3 * (level - 1) + slot
             ref = pieces.at[level - 1, slot, :, half_rows, lanes]
             arrived(ref, plane_recv.at[part, at])
+            if level == 2 and isinstance(slot, int):
+                remote(
+                    ref, pieces.at[1, 1 - chip_odd, :, half_rows, lanes],
+                    plane_send.at[part, 9], plane_recv.at[part, 4 - chip_odd], beside,
+                )
             remote(ref, ref, twin_send.at[part, at], twin_recv.at[part, at], twin)
 
     def pass_on_first(part):
@@ -456,8 +473,19 @@
                     piece_grad[level - 1, slot, kv, half_rows, lanes].astype(f32)
                     + twin_grad[level - 2, slot, kv, :, lanes].astype(f32)
                 ).astype(bf16)
+        if level == 2:
+            remote(
+                piece_grad.at[1, chip_odd, :, half_rows, lanes], relayed.at[:, :, lanes],
+                gplane_send.at[part, 10], gplane_recv.at[part, 6], beside,
+            )
+            remote(
+                piece_grad.at[1, 1 - chip_odd, :, half_rows, lanes],
+                coarse_in.at[:, pl.ds(contribution_base(2), 64), lanes],
+                gplane_send.at[part, 11], gplane_recv.at[part, 1], two_back,
+            )
+            return
         targets = group_targets(level)
-        place = {4: 1, 3: 4, 2: 10}[level]
+        place = {4: 1, 3: 4}[level]
         for slot in range(3):
             for chip in range(plane_chips(level)):
                 if level == 4:
@@ -479,6 +507,20 @@
                     )
                 place += 1
 
+    def relay_to_owner(part):
+        lanes = group_lanes(part)
+        arrived(relayed.at[:, :, lanes], gplane_recv.at[part, 6])
+        for kv in range(2):
+            piece_grad[1, 2, kv, half_rows, lanes] = (
+                piece_grad[1, 2, kv, half_rows, lanes].astype(f32)
+                + relayed[kv, :, lanes].astype(f32)
+            ).astype(bf16)
+        remote(
+            piece_grad.at[1, 2, :, half_rows, lanes],
+            coarse_in.at[:, pl.ds(contribution_base(2) + 64, 64), lanes],
+            gplane_send.at[part, 12], gplane_recv.at[part, 7], group_targets(2)[2] + core,
+        )
+
     def first_to_owner(part):
         lanes = group_lanes(part)
         arrived(twin_first.at[0, :, :, lanes], gtwin_recv.at[part, 0])
@@ -542,9 +584,8 @@
         lanes = group_lanes(part)
         arrived(near_in.at[0, :, :, lanes], gnear_recv.at[part, 0])
         arrived(near_in.at[1, :, :, lanes], gnear_recv.at[part, 1])
-        for level in range(1, LEVELS):
-            base, width = contribution_base(level), contribution_width(level)
-            arrived(coarse_in.at[:, pl.ds(base, width), lanes], gplane_recv.at[part, level - 1])
+        for base, width, sem in ((0, 128, 0), (128, 64, 1), (192, 64, 7), (256, 192, 2)):
+            arrived(coarse_in.at[:, pl.ds(base, width), lanes], gplane_recv.at[part, sem])
         for step in (1, 3, 2):
             base = contribution_base(4) + lax.rem(row_place + 4 - step, 4) * 16
             arrived(
@@ -576,15 +617,16 @@
     first_to_owner(0)
     backward_far(0)
     grads_to_owners(0, 4)
+    backward_level(0, 2)
+    backward_level(0, 3)
+    grads_to_owners(0, 2)
     pass_on(1, 3)
-    backward_level(0, 3)
     pass_on(1, 2)
-    backward_level(0, 2)
+    backward_twin(0)
     grads_to_owners(0, 3)
+    relay_to_owner(0)
     pass_on(1, 4)
     pass_on_first(1)
-    backward_twin(0)
-    grads_to_owners(0, 2)
     forward_level(1, 3)
     forward_level(1, 2)
     forward_level(1, 4)
@@ -598,11 +640,12 @@
     first_to_owner(1)
     backward_far(1)
     grads_to_owners(1, 4)
+    backward_level(1, 2)
     backward_level(1, 3)
-    backward_level(1, 2)
+    grads_to_owners(1, 2)
+    backward_twin(1)
     grads_to_owners(1, 3)
-    backward_twin(1)
-    grads_to_owners(1, 2)
+    relay_to_owner(1)
     backward_own(1)
     write(0)
     row_to_owners(1)
@@ -662,11 +705,12 @@
         pltpu.VMEM((3, 2, 64, FEATURES), bf16),
         pltpu.VMEM((2, 64, FEATURES), bf16),
         pltpu.VMEM((2, 128, FEATURES), bf16),
+        pltpu.VMEM((2, 64, FEATURES), bf16),
         dma((2, 2)), dma((2, 2)),
         dma((2, plane_messages)), dma((2, 3 * LEVELS)),
         dma((2, 3 * LEVELS)), dma((2, 3 * LEVELS)),
         dma((2, 2)), dma((2, 2)),
-        dma((2, plane_messages)), dma((2, LEVELS + 2)),
+        dma((2, plane_messages)), dma((2, LEVELS + 4)),
         dma((2, 3 * LEVELS)), dma((2, 3 * LEVELS)),
         dma((3,)), dma((3,)), dma((2, 3)), dma((2, 3)),
     ]

time: 79.4 us -> 82.9 us (1.044); the launches traced: 79.3 us -> 81.8 us
  Pallas kernels: 78.5 us -> 81 us
    pallas_call x1, Pallas kernels: 76.5 us -> 79 us  [on_device(): pl.pallas_call(functools.partial(kernel, device_count, sub_count), out_sh...]
where the time goes in v3:
time: 82.9 us; the launch traced here: 81.8 us
  Pallas kernels  81 us (98%)
    pallas_call x1, Pallas kernels, on_device(): pl.pallas_call(functools.partial(kernel, device_count, sub_count), out_sh...  79 us
    pallas_call x1, Pallas kernels, on_device(): pl.pallas_call(hand_over, out_shape=[jax.ShapeDtypeStruct(rows, bf16)] *...  1.98 us

profile of v3, /device:TPU:3, one launch (start us, length us, event | category | flops | bytes accessed | tf_op | source)
XLA Modules:
  0.0 81.8 jit_solution(17294465103336262725)
XLA Ops:
  0.6 79.0 %hierarchical_attention.1 = (bf16[256,512]{1,0:T(8,128)(2,1)}, bf16[256,512]{1,0:T(8,128)(2,1)}, bf16[256,512]{1,0:T(8,128)(2,1)}, bf16[256,512]{1,0:T(8,128)(2,1)}) custom-call(bf16[256,512]{1,0:T(8,128)(2,1)} %q_ref.1, bf16[256,512]{1,0:T(8,128)(2,1)} %k_ref.1, bf16[256,512]{1,0:T(8,128)(2,1)} %v_ref.1, bf16[256,512]{1,0:T(8,128)(2,1)} %g_ref.1), custom_call_target="tpu_custom_call" | custom-call | tf_op jit(solution)/shard_map/hierarchical_attention/pallas_call | solution.py:717
  79.6 2.0 %hand_over.1 = (bf16[256,512]{1,0:T(8,128)(2,1)}, bf16[256,512]{1,0:T(8,128)(2,1)}, bf16[256,512]{1,0:T(8,128)(2,1)}, bf16[256,512]{1,0:T(8,128)(2,1)}) custom-call(bf16[256,512]{1,0:T(8,128)(2,1)} %get-tuple-element.8.refs_0_, bf16[256,512]{1,0:T(8,128)(2,1)} %get-tuple-element.9.refs_1_, bf16[256,512]{1,0:T(8,128)(2,1)} %get-tuple-element.10.refs_2_, ...), custom_call_target="tpu_custom_call" | custom-call | tf_op jit(solution)/shard_map/hand_over/pallas_call | solution.py:729

commit v4 on v2

--- a/solution.py
+++ b/solution.py
@@ -159,7 +159,7 @@
         pltpu.make_async_copy(ref, ref, sem).wait()
 
     def group_lanes(part):
-        return pl.ds(part * 256, 256)
+        return pl.ds(384, 128) if part else pl.ds(0, 384)
 
     for step in (1, 3, 2):
         remote(
@@ -220,14 +220,14 @@
             row_keys.at[:, pl.ds(pl.multiple_of(from_place * 16, 16), 16)], row_recv.at[step - 1]
         )
     send_row(0)
+    send_row(1)
     send_keys(1)
-    send_row(1)
 
     lane = lax.broadcasted_iota(jnp.int32, (BLOCK, 128), 1)
     first_head = lane < 64
 
     def pairs_of(part):
-        return range(2 * part, 2 * part + 2)
+        return range(3, 4) if part else range(3)
 
     def pair_lanes(pair):
         return slice(pair * 128, pair * 128 + 128)
@@ -576,15 +576,15 @@
     first_to_owner(0)
     backward_far(0)
     grads_to_owners(0, 4)
-    pass_on(1, 3)
     backward_level(0, 3)
-    pass_on(1, 2)
     backward_level(0, 2)
     grads_to_owners(0, 3)
+    pass_on(1, 3)
+    pass_on(1, 2)
+    backward_twin(0)
+    grads_to_owners(0, 2)
     pass_on(1, 4)
     pass_on_first(1)
-    backward_twin(0)
-    grads_to_owners(0, 2)
     forward_level(1, 3)
     forward_level(1, 2)
     forward_level(1, 4)
@@ -603,9 +603,9 @@
     grads_to_owners(1, 3)
     backward_twin(1)
     grads_to_owners(1, 2)
+    row_to_owners(1)
     backward_own(1)
     write(0)
-    row_to_owners(1)
     write(1)
     for copy in started:
         copy.wait_send()

time: 79.4 us -> 83.8 us (1.055)
  Pallas kernels: 78.5 us -> 82.9 us
    pallas_call x1, Pallas kernels: 76.5 us -> 80.9 us  [on_device(): pl.pallas_call(functools.partial(kernel, device_count, sub_count), out_sh...]
where the time goes in v4:
time: 83.8 us; the launch traced here: 83.7 us
  Pallas kernels  82.9 us (99%)
    pallas_call x1, Pallas kernels, on_device(): pl.pallas_call(functools.partial(kernel, device_count, sub_count), out_sh...  80.9 us
    pallas_call x1, Pallas kernels, on_device(): pl.pallas_call(hand_over, out_shape=[jax.ShapeDtypeStruct(rows, bf16)] *...  1.98 us

profile of v4, /device:TPU:3, one launch (start us, length us, event | category | flops | bytes accessed | tf_op | source)
XLA Modules:
  0.0 83.7 jit_solution(11651481026089810188)
XLA Ops:
  0.6 80.9 %hierarchical_attention.1 = (bf16[256,512]{1,0:T(8,128)(2,1)}, bf16[256,512]{1,0:T(8,128)(2,1)}, bf16[256,512]{1,0:T(8,128)(2,1)}, bf16[256,512]{1,0:T(8,128)(2,1)}) custom-call(bf16[256,512]{1,0:T(8,128)(2,1)} %q_ref.1, bf16[256,512]{1,0:T(8,128)(2,1)} %k_ref.1, bf16[256,512]{1,0:T(8,128)(2,1)} %v_ref.1, bf16[256,512]{1,0:T(8,128)(2,1)} %g_ref.1), custom_call_target="tpu_custom_call" | custom-call | tf_op jit(solution)/shard_map/hierarchical_attention/pallas_call | solution.py:673
  81.5 2.0 %hand_over.1 = (bf16[256,512]{1,0:T(8,128)(2,1)}, bf16[256,512]{1,0:T(8,128)(2,1)}, bf16[256,512]{1,0:T(8,128)(2,1)}, bf16[256,512]{1,0:T(8,128)(2,1)}) custom-call(bf16[256,512]{1,0:T(8,128)(2,1)} %get-tuple-element.8.refs_0_, bf16[256,512]{1,0:T(8,128)(2,1)} %get-tuple-element.9.refs_1_, bf16[256,512]{1,0:T(8,128)(2,1)} %get-tuple-element.10.refs_2_, ...), custom_call_target="tpu_custom_call" | custom-call | tf_op jit(solution)/shard_map/hand_over/pallas_call | solution.py:685
